TPU v7x, 32 devices: a whole 2x2x4 slice. The times are simulated.
32 devices in a mesh: seq: 8 (over y, x, core), head: 4 (over z).
Axes of the slice: x: 2, y: 2, z: 4, core: 2. Of those that a mesh axis runs over, the one named last changes fastest.
Arguments:
- activations: bfloat16 [4096, 5376], P(('seq', 'head')), may hold values from -42 to 42, as said below
- input_gain: float32 [5376], replicated, may hold values from 0.1 to 1.9
- query_weight: bfloat16 [5376, 4096], P(None, 'head'), may hold values from -2.2818633 to 2.2818633
- key_weight: bfloat16 [5376, 2048], P(None, 'head'), may hold values from -1 to 1
- value_weight: bfloat16 [5376, 2048], P(None, 'head'), may hold values from -0.078125 to 0.078125
- output_weight: bfloat16 [4096, 5376], P('head'), may hold values from -0.09375 to 0.09375
- cache_edge: bfloat16 [2, 1024, 2048], P(None, None, 'head'), may hold values from -6 to 6
- post_gain: float32 [5376], replicated, may hold values from 0.1 to 1.9
Outputs:
- layer_out: bfloat16 [4096, 5376], P(('seq', 'head'))
Inputs may be any that keep to these rules, and one draw needn't show every extreme that they name: `activations`: input rows with row and feature scales.
All inputs are finite; a program needn't handle non-finite values.
Results may differ from a plain program's by a relative error of at most 0.006.
Values may be sent and summed in bfloat16 or wider, within the bound.
A program may use at most 128 MiB of HBM per device.

v0:
```python
import jax
import jax.numpy as jnp
from jax import lax
from jax.sharding import PartitionSpec as P

HD = 128
WINDOW = 1024
SCALAR = 168
TOK_DEV = 512
EPSILON = 1e-06
ROPE_BASE = 10000.0


def from_behind(array, axis, by):
    count = lax.axis_size(axis)
    pairs = [(i, i + by) for i in range(count) if 0 <= i + by < count]
    return lax.ppermute(array, axis, pairs)


def normalize_rows(values, gain):
    return values * lax.rsqrt(jnp.mean(values * values, axis=-1, keepdims=True) + EPSILON) * gain


def rotate(vectors, positions):
    half_size = vectors.shape[-1] // 2
    frequency = ROPE_BASE ** (-(jnp.arange(half_size, dtype=jnp.float32) * 2.0 / vectors.shape[-1]))
    angles = positions[:, None] * frequency[None, :]
    cosine = jnp.cos(angles)[:, None, :]
    sine_part = jnp.sin(angles)[:, None, :]
    first_half = vectors[..., :half_size]
    second_half = vectors[..., half_size:]
    return jnp.concatenate(
        [
            first_half * cosine - second_half * sine_part,
            second_half * cosine + first_half * sine_part,
        ],
        axis=-1,
    )


def per_device(
    activations,
    input_gain,
    query_weight,
    key_weight,
    value_weight,
    output_weight,
    cache_edge,
    post_gain,
):
    heads_query = query_weight.shape[1] // HD
    heads_kv = key_weight.shape[1] // HD
    group_size = heads_query // heads_kv
    query_width = heads_query * HD
    kv_width = heads_kv * HD
    seq_pos = lax.axis_index("seq")
    first_pos = seq_pos * TOK_DEV
    normed = normalize_rows(activations.astype(jnp.float32), input_gain).astype(jnp.bfloat16)
    normed = lax.all_gather(normed, "head", axis=0, tiled=True)
    row_count = normed.shape[0]
    positions = (first_pos + jnp.arange(row_count, dtype=jnp.int32)).astype(jnp.float32)
    queries_raw = jnp.dot(normed, query_weight, preferred_element_type=jnp.float32)
    keys_raw = jnp.dot(normed, key_weight, preferred_element_type=jnp.float32)
    value_rows = jnp.dot(normed, value_weight, preferred_element_type=jnp.float32)
    queries = rotate(queries_raw.reshape(row_count, heads_query, HD), positions) * SCALAR ** (-0.5)
    keys = rotate(keys_raw.reshape(row_count, heads_kv, HD), positions)
    joined = jnp.concatenate(
        [queries.reshape(row_count, query_width), keys.reshape(row_count, kv_width), value_rows],
        axis=1,
    )
    packed = joined.astype(jnp.bfloat16)
    queries = packed[:, :query_width]
    own_edge = packed[:, query_width:]
    cache_rows = jnp.concatenate([cache_edge[0], cache_edge[1]], axis=1)
    reach_steps = WINDOW // TOK_DEV
    earlier = []
    received = own_edge
    for distance in range(1, reach_steps + 1):
        received = from_behind(own_edge, "seq", distance)
        offset = jnp.clip(WINDOW + (seq_pos - distance) * TOK_DEV, 0, WINDOW - TOK_DEV)
        from_cache = lax.dynamic_slice_in_dim(cache_rows, offset, TOK_DEV, 0)
        earlier.append(jnp.where(seq_pos >= distance, received, from_cache))
    window_rows = jnp.concatenate(earlier[::-1] + [own_edge], axis=0)
    span_length = window_rows.shape[0]
    key_rows = window_rows[:, :kv_width].reshape(span_length, heads_kv, HD)
    value_block = window_rows[:, kv_width:].reshape(span_length, heads_kv, HD)
    query_block = queries.reshape(TOK_DEV, heads_kv, group_size, HD)
    query_index = jnp.arange(TOK_DEV, dtype=jnp.int32)
    key_index = jnp.arange(span_length, dtype=jnp.int32)
    allowed = (key_index[None, :] > query_index[:, None]) & (
        key_index[None, :] <= query_index[:, None] + WINDOW
    )
    scores = jnp.einsum("qgrd,kgd->grqk", query_block, key_rows, preferred_element_type=jnp.float32)
    scores = jnp.where(allowed[None, None], scores, -jnp.inf)
    largest = jnp.max(scores, axis=-1, keepdims=True)
    exps = jnp.exp(scores - largest)
    probabilities = (exps / jnp.sum(exps, axis=-1, keepdims=True)).astype(jnp.bfloat16)
    attended = jnp.einsum(
        "grqk,kgd->qgrd", probabilities, value_block, preferred_element_type=jnp.float32
    )
    attended = attended.astype(jnp.bfloat16).reshape(TOK_DEV, query_width)
    projected = lax.psum_scatter(
        jnp.dot(attended, output_weight, preferred_element_type=jnp.float32).astype(jnp.bfloat16),
        "head",
        scatter_dimension=0,
        tiled=True,
    ).astype(jnp.float32)
    branch = normalize_rows(projected, post_gain)
    return (activations.astype(jnp.float32) + branch).astype(jnp.bfloat16)


def solution(mesh):
    return jax.shard_map(
        per_device,
        mesh=mesh,
        in_specs=(
            P(("seq", "head"), None),
            P(),
            P(None, "head"),
            P(None, "head"),
            P(None, "head"),
            P("head", None),
            P(None, None, "head"),
            P(),
        ),
        out_specs=P(("seq", "head"), None),
        check_vma=False,
    )
```

profile of v0, /device:TPU:0, one launch (start us, length us, event | category | flops | bytes accessed | tf_op | source)
XLA Modules:
  0.0 335.1 jit_solution(6270335785261173082)
XLA Ops:
  6.5 0.0 all-gather.2.cloned.1.call-start
  6.5 1.7 fusion.10
  8.2 2.8 fusion.12
  11.0 0.0 all-gather.2.cloned.1.call-update
  11.1 0.0 reduce-scatter.2.cloned.1.call-start
  11.2 0.5 multiply_cosine_fusion
  11.7 0.8 copy.11
  12.5 0.8 copy.12
  13.4 1.7 fusion.24
  15.0 0.5 copy.22
  15.6 0.5 copy.21
  16.1 1.5 fusion.7
  17.6 98.7 %all-gather.2.cloned.1.call-done = bf16[512,5376]{1,0:T(8,128)(2,1)} async-done(((bf16[128,5376]{1,0:T(8,128)(2,1)}), bf16[512,5376]{1,0:T(8,128)(2,1)}) %all-gather.2.cloned.1.call-update) | async-done | bytes 5505040 | tf_op jit(solution)/shard_map/all_gather | solution.py:59
  116.3 0.0 copy-start.4
  116.3 7.3 %fusion.26 = f32[512,512]{0,1:T(8,128)S(1)} fusion(bf16[512,5376]{1,0:T(8,128)(2,1)} %all-gather.2.cloned.1.call-done, bf16[5376,512]{1,0:T(8,128)(2,1)} %param.11), kind=kOutput, calls=%fused_computation.56 | convolution fusion | flops 2818572288 | bytes 12058624 | tf_op jit(solution)/shard_map/dot_general | solution.py:63
  123.7 0.2 subtract_convert_fusion
  123.8 0.0 slice-start
  123.9 0.0 copy-done.4
  123.9 0.0 slice-start.1
  123.9 0.0 slice-start.2
  123.9 5.8 %convolution_convert_fusion.1 = bf16[512,512]{0,1:T(8,128)(2,1)S(1)} fusion(bf16[512,5376]{1,0:T(8,128)(2,1)S(1)} %copy-done.4, bf16[5376,512]{1,0:T(8,128)(2,1)} %param.12), kind=kOutput, calls=%fused_computation.35 | convolution fusion | flops 2818834432 | bytes 11534336 | tf_op jit(solution)/shard_map/dot_general | solution.py:64
  129.7 0.1 pad_maximum_fusion
  129.8 2.0 collective-permute-start.1
  131.8 3.8 %collective-permute-start = (bf16[512,1024]{0,1:T(8,128)(2,1)S(1)}, bf16[512,1024]{0,1:T(8,128)(2,1)S(1)}, u32[]{:S(2)}, u32[]{:S(2)}) collective-permute-start(bf16[512,1024]{0,1:T(8,128)(2,1)S(1)} %pad_maximum_fusion), channel_id=1, source_target_pairs={{0,8},{4,12},{8,16},{12,20},{16,24},{20,28},{1,9},{5,13},{9,17},{1... | collective-permute-start | bytes 3145736 | tf_op jit(solution)/shard_map/ppermute | solution.py:17
  135.6 0.0 slice-done
  135.6 0.0 slice-done.1
  135.7 0.0 slice-done.2
  135.7 5.8 %convolution_bitcast_fusion = f32[64,8,8,128]{3,1,2,0:T(8,128)S(1)} fusion(bf16[512,5376]{1,0:T(8,128)(2,1)S(1)} %copy-done.4, bf16[5376,1024]{1,0:T(8,128)(2,1)S(1)} %bitcast.59), kind=kOutput, calls=%fused_computation.33 | convolution fusion | flops 5637144576 | bytes 18612224 | tf_op jit(solution)/shard_map/dot_general | solution.py:62
  141.5 0.0 copy-start.1
  141.5 0.0 copy-start.2
  141.5 0.5 copy.23
  142.0 0.4 copy-done.1
  142.5 0.1 copy-done.2
  142.5 1.1 multiply_subtract_fusion
  143.6 0.6 fusion.14
  144.2 0.1 copy.13
  144.4 0.0 collective-permute-done.1
  144.4 14.3 %collective-permute-done = bf16[512,1024]{0,1:T(8,128)(2,1)S(1)} collective-permute-done((bf16[512,1024]{0,1:T(8,128)(2,1)S(1)}, bf16[512,1024]{0,1:T(8,128)(2,1)S(1)}, u32[]{:S(2)}, u32[]{:S(2)}) %collective-permute-start) | collective-permute-done | bytes 1048608 | tf_op jit(solution)/shard_map/ppermute | solution.py:17
  158.7 2.2 fusion.19
  160.9 9.5 %maximum_maximum_fusion = bf16[1536,1024]{0,1:T(8,128)(2,1)S(1)} fusion(bf16[512,512]{0,1:T(8,128)(2,1)S(1)} %convolution_convert_fusion.1, bf16[512,512]{0,1:T(8,128)(2,1)S(1)} %bitcast.51, bf16[512,1024]{0,1:T(8,128)(2,1)S(1)} %get-tuple-element.10, bf16[512,1024]{0,1:T(8,128)(2,1)S(1)} %get-tuple-element.9), kind=kLoop, calls=%fused_computation.15 | loop fusion | flops 12582912 | bytes 6291456 | tf_op jit(solution)/shard_map/concatenate | solution.py:83
  170.4 1.4 fusion.23
  171.8 11.8 %fusion.27 = f32[4,1536,512,2]{2,1,3,0:T(8,128)} fusion(bf16[1536,4,128,1]{0,2,3,1:T(8,128)(2,1)S(1)} %bitcast.48, bf16[512,4,2,128]{3,0,2,1:T(8,128)(2,1)S(1)} %bitcast.54), kind=kOutput, calls=%fused_computation.57 | convolution fusion | flops 1610612736 | bytes 27787264 | tf_op jit(solution)/shard_map/qgrd,kgd->grqk/dot_general | solution.py:93
  183.6 9.2 %fusion.25 = f32[4,2,512]{2,1,0:T(2,128)S(1)} fusion(pred[512,1536]{0,1:T(8,128)(4,1)} %fusion.7, bf16[1536,4,128,1]{0,2,3,1:T(8,128)(2,1)S(1)} %bitcast.49, bf16[512,4,2,128]{3,0,2,1:T(8,128)(2,1)S(1)} %bitcast.55), kind=kOutput, calls=%fused_computation.55 | convolution fusion | flops 1629488640 | bytes 3424256 | tf_op jit(solution)/shard_map/sub | solution.py:96
  192.8 13.0 %fusion.15 = bf16[4,128,2,512]{3,1,2,0:T(8,128)(2,1)S(1)} fusion(bf16[1536,4,128,1]{0,2,3,1:T(8,128)(2,1)} %bitcast.56, f32[4,2,512]{2,1,0:T(2,128)S(1)} %fusion.25, f32[4,1536,512,2]{2,1,3,0:T(8,128)} %fusion.27, pred[512,1536]{0,1:T(8,128)(4,1)} %fusion.7), kind=kOutput, calls=%fused_computation.34 | convolution fusion | flops 1636308480 | bytes 28590080 | tf_op jit(solution)/shard_map/grqk,kgd->qgrd/dot_general | solution.py:98
  205.8 11.9 %convolution_convert_fusion = bf16[512,5376]{1,0:T(8,128)(2,1)} fusion(bf16[512,1024]{0,1:T(8,128)(2,1)S(1)} %bitcast.60, bf16[1024,5376]{1,0:T(8,128)(2,1)} %param.13), kind=kOutput, calls=%fused_computation.8 | convolution fusion | flops 5639897088 | bytes 17563648 | tf_op jit(solution)/shard_map/dot_general | solution.py:103
  217.6 0.0 copy-start
  217.6 0.0 copy-start.3
  217.6 0.0 reduce-scatter.2.cloned.1.call-update
  217.7 105.6 %reduce-scatter.2.cloned.1.call-done = bf16[128,5376]{1,0:T(8,128)(2,1)} async-done(((bf16[512,5376]{1,0:T(8,128)(2,1)}), bf16[128,5376]{1,0:T(8,128)(2,1)}) %reduce-scatter.2.cloned.1.call-update) | async-done | bytes 1376272 | tf_op jit(solution)/shard_map/reduce_scatter | solution.py:102
  323.3 1.7 fusion.8
  325.0 0.0 copy-done
  325.0 0.0 copy-done.3
  325.0 3.0 fusion.13
  (7 shorter events, 0.1 us)
Async XLA Ops:
  6.5 109.8 %all-gather.2.cloned.1.call-start = ((), (), s32[]{:S(2)}) async-start(), calls=%async_computation.1 | async-start | bytes 6881280 | tf_op jit(solution)/shard_map/all_gather | solution.py:59
  11.1 312.2 %reduce-scatter.2.cloned.1.call-start = ((), (), s32[]{:S(2)}) async-start(), calls=%async_computation.2 | async-start | bytes 6881280 | tf_op jit(solution)/shard_map/reduce_scatter | solution.py:102
  116.3 7.6 %copy-start.4 = (bf16[512,5376]{1,0:T(8,128)(2,1)S(1)}, bf16[512,5376]{1,0:T(8,128)(2,1)}, u32[]{:S(2)}) copy-start(bf16[512,5376]{1,0:T(8,128)(2,1)} %all-gather.2.cloned.1.call-done) | copy-start | bytes 16515076
  123.8 11.8 %slice-start = ((s8[11010048]{0:T(1024)(128)(4,1)}), s8[4194304]{0:T(1024)(128)(4,1)S(1)}, s32[]{:S(2)}) async-start(s8[11010048]{0:T(1024)(128)(4,1)} %bitcast.58), calls=%async_computation.3 | async-start | bytes 8388608
  123.9 11.7 %slice-start.1 = ((s8[11010048]{0:T(1024)(128)(4,1)}), s8[4194304]{0:T(1024)(128)(4,1)S(1)}, s32[]{:S(2)}) async-start(s8[11010048]{0:T(1024)(128)(4,1)} %bitcast.58), calls=%async_computation.4 | async-start | bytes 8388608
  123.9 11.7 %slice-start.2 = ((s8[11010048]{0:T(1024)(128)(4,1)}), s8[2621440]{0:T(1024)(128)(4,1)S(1)}, s32[]{:S(2)}) async-start(s8[11010048]{0:T(1024)(128)(4,1)} %bitcast.58), calls=%async_computation.5 | async-start | bytes 5242880
  129.8 14.6 %collective-permute-start.1 = (bf16[512,1024]{0,1:T(8,128)(2,1)S(1)}, bf16[512,1024]{0,1:T(8,128)(2,1)S(1)}, u32[]{:S(2)}, u32[]{:S(2)}) collective-permute-start(bf16[512,1024]{0,1:T(8,128)(2,1)S(1)} %pad_maximum_fusion), channel_id=1, source_target_pairs={{0,4},{4,8},{8,12},{12,16},{16,20},{20,24},{24,28},{1,5},{5,9},{9,... | collective-permute-start | bytes 3145736 | tf_op jit(solution)/shard_map/ppermute | solution.py:17
  131.8 26.9 %collective-permute-start = (bf16[512,1024]{0,1:T(8,128)(2,1)S(1)}, bf16[512,1024]{0,1:T(8,128)(2,1)S(1)}, u32[]{:S(2)}, u32[]{:S(2)}) collective-permute-start(bf16[512,1024]{0,1:T(8,128)(2,1)S(1)} %pad_maximum_fusion), channel_id=1, source_target_pairs={{0,8},{4,12},{8,16},{12,20},{16,24},{20,28},{1,9},{5,13},{9,17},{1... | collective-permute-start | bytes 3145736 | tf_op jit(solution)/shard_map/ppermute | solution.py:17
  141.5 1.0 copy-start.1
  141.5 1.0 copy-start.2
  217.6 107.4 %copy-start = (bf16[128,5376]{1,0:T(8,128)(2,1)S(1)}, bf16[128,5376]{1,0:T(8,128)(2,1)}, u32[]{:S(2)}) copy-start(bf16[128,5376]{1,0:T(8,128)(2,1)} %param.8) | copy-start | bytes 4128772
  217.6 107.4 %copy-start.3 = (f32[5376]{0:T(1024)S(1)}, f32[5376]{0:T(1024)}, u32[]{:S(2)}) copy-start(f32[5376]{0:T(1024)} %param.15) | copy-start | bytes 64516
Sparse Core Ops, SparseCore 0:
  11.2 105.0 all-gather.1
  217.8 105.4 reduce-scatter.1
where the time goes:
time: 341 us; the launch traced here: 335 us
  waiting for transfers between devices  219 us (64%)
  matrix products  64.7 us (19%)
  other arithmetic  24.8 us (7%)
  between operations  13.9 us (4%)
  local copies, waits for them, and re-layouts  7 us (2%)
  starting transfers between devices  5.89 us (2%)
    reduce_scatter x1, waiting for transfers between devices, per_device(): lax.psum_scatter(jnp.dot(attended, output_weight, preferred_element_type=...  106 us
    all_gather x1, waiting for transfers between devices, per_device(): normed = lax.all_gather(normed, 'head', axis=0, tiled=True)  98.7 us
    ppermute x2, waiting for transfers between devices, from_behind(): return lax.ppermute(array, axis, pairs)  14.3 us
    dot_general x1, matrix products, per_device(): jnp.einsum('grqk,kgd->qgrd', probabilities, value_block, preferred_elemen...  13 us
    dot_general x1, matrix products, per_device(): jnp.dot(attended, output_weight, preferred_element_type=jnp.float32)  11.9 us
    dot_general x1, matrix products, per_device(): jnp.einsum('qgrd,kgd->grqk', query_block, key_rows, preferred_element_typ...  11.8 us
    concatenate x1, other arithmetic, per_device(): window_rows = jnp.concatenate(earlier[::-1] + [own_edge], axis=0)  9.49 us
    sub x1, matrix products, per_device(): exps = jnp.exp(scores - largest)  9.22 us
  transfers between devices with their start and end apart: 4, of which 3 were waited for; matrix products, arithmetic and copies ran while one was open for 4% of the time, Pallas kernels for 0%

commit v1 on v0

--- a/solution.py
+++ b/solution.py
@@ -56,7 +56,12 @@
     seq_pos = lax.axis_index("seq")
     first_pos = seq_pos * TOK_DEV
     normed = normalize_rows(activations.astype(jnp.float32), input_gain).astype(jnp.bfloat16)
-    normed = lax.all_gather(normed, "head", axis=0, tiled=True)
+    ring = [normed]
+    for hop in range(3):
+        ring.append(lax.ppermute(ring[-1], "head", [(dev, (dev + 1) % 4) for dev in range(4)]))
+    normed = jnp.roll(
+        jnp.concatenate(ring[::-1], axis=0), (lax.axis_index("head") + 1) * ring[0].shape[0], axis=0
+    )
     row_count = normed.shape[0]
     positions = (first_pos + jnp.arange(row_count, dtype=jnp.int32)).astype(jnp.float32)
     queries_raw = jnp.dot(normed, query_weight, preferred_element_type=jnp.float32)

time: 341 us -> 332 us (0.974); the launches traced: 335 us -> 332 us
  waiting for transfers between devices: 219 us -> 206 us
  local copies, waits for them, and re-layouts: 7 us -> 14.2 us
    all_gather x1 -> x0, waiting for transfers between devices: 98.7 us -> none  [per_device(): normed = lax.all_gather(normed, 'head', axis=0, tiled=True)]
    ppermute x0 -> x3, waiting for transfers between devices: none -> 87.9 us  [per_device(): lax.ppermute(ring[-1], 'head', [(dev, (dev + 1) % 4) for dev in range(4)])]
    unnamed x19 -> x25, local copies, waits for them, and re-layouts: 2.11 us -> 9.39 us
  transfers between devices with their start and end apart: 4 -> 6, of which waited for: 3 -> 5; matrix products, arithmetic and copies ran while one was open for 4% -> 6% of each run, Pallas kernels for 0% -> 0%
where the time goes in v1:
time: 332 us
  waiting for transfers between devices  206 us (62%)
  matrix products  65.4 us (20%)
  other arithmetic  24.6 us (7%)
  local copies, waits for them, and re-layouts  14.2 us (4%)
  between operations  13.7 us (4%)
  starting transfers between devices  8.15 us (2%)
    reduce_scatter x1, waiting for transfers between devices, per_device(): lax.psum_scatter(jnp.dot(attended, output_weight, preferred_element_type=...  105 us
    ppermute x3, waiting for transfers between devices, per_device(): lax.ppermute(ring[-1], 'head', [(dev, (dev + 1) % 4) for dev in range(4)])  87.9 us
    dot_general x1, matrix products, per_device(): jnp.einsum('grqk,kgd->qgrd', probabilities, value_block, preferred_elemen...  13 us
    ppermute x2, waiting for transfers between devices, from_behind(): return lax.ppermute(array, axis, pairs)  12.4 us
    dot_general x1, matrix products, per_device(): jnp.dot(attended, output_weight, preferred_element_type=jnp.float32)  12.1 us
    dot_general x1, matrix products, per_device(): jnp.einsum('qgrd,kgd->grqk', query_block, key_rows, preferred_element_typ...  11.8 us
    concatenate x1, other arithmetic, per_device(): window_rows = jnp.concatenate(earlier[::-1] + [own_edge], axis=0)  9.52 us
    unnamed x25, local copies, waits for them, and re-layouts  9.39 us
  transfers between devices with their start and end apart: 6, of which 5 were waited for; matrix products, arithmetic and copies ran while one was open for 6% of the time, Pallas kernels for 0%

profile of v1, /device:TPU:0, one launch (start us, length us, event | category | flops | bytes accessed | tf_op | source)
XLA Modules:
  0.0 331.7 jit_solution(16539235749469659145)
XLA Ops:
  6.5 0.0 reduce-scatter.2.cloned.1.call-start
  6.5 1.7 fusion.16
  8.2 1.7 fusion.18
  10.0 3.1 collective-permute-start
  13.0 32.2 %collective-permute-done = bf16[128,5376]{1,0:T(8,128)(2,1)S(1)} collective-permute-done((bf16[128,5376]{1,0:T(8,128)(2,1)S(1)}, bf16[128,5376]{1,0:T(8,128)(2,1)S(1)}, u32[]{:S(2)}, u32[]{:S(2)}) %collective-permute-start) | collective-permute-done | bytes 1376288 | tf_op jit(solution)/shard_map/ppermute | solution.py:61
  45.3 0.0 collective-permute-start.1
  45.3 33.2 %collective-permute-done.1 = bf16[128,5376]{1,0:T(8,128)(2,1)S(1)} collective-permute-done((bf16[128,5376]{1,0:T(8,128)(2,1)S(1)}, bf16[128,5376]{1,0:T(8,128)(2,1)S(1)}, u32[]{:S(2)}, u32[]{:S(2)}) %collective-permute-start.1) | collective-permute-done | bytes 1376288 | tf_op jit(solution)/shard_map/ppermute | solution.py:61
  78.4 0.0 copy-start.1
  78.4 0.0 collective-permute-start.2
  78.4 0.5 multiply_cosine_fusion
  79.0 0.1 copy.11
  79.1 0.1 copy.12
  79.3 3.0 fusion.39
  82.2 2.3 copy.22
  84.5 0.0 copy-done.1
  84.5 2.3 copy.21
  86.8 0.0 copy-start.2
  86.8 1.5 fusion.13
  88.3 22.5 %collective-permute-done.2 = bf16[128,5376]{1,0:T(8,128)(2,1)} collective-permute-done((bf16[128,5376]{1,0:T(8,128)(2,1)S(1)}, bf16[128,5376]{1,0:T(8,128)(2,1)}, u32[]{:S(2)}, u32[]{:S(2)}) %collective-permute-start.2) | collective-permute-done | bytes 1376288 | tf_op jit(solution)/shard_map/ppermute | solution.py:61
  110.8 1.4 constant_dynamic-update-slice_fusion.7
  112.2 0.0 copy-done.2
  112.2 0.0 copy-start
  112.2 0.0 copy-start.6
  112.2 0.1 constant_dynamic-update-slice_fusion.6
  112.3 0.1 constant_dynamic-update-slice_fusion.5
  112.4 1.1 copy-done
  113.6 0.0 copy-done.6
  113.6 0.4 constant_dynamic-update-slice_fusion.4
  113.9 1.4 constant_dynamic-update-slice_fusion.3
  115.4 0.1 constant_dynamic-update-slice_fusion.2
  115.5 0.1 constant_dynamic-update-slice_fusion.1
  115.6 0.4 constant_dynamic-update-slice_fusion
  116.0 5.6 %fusion.25 = bf16[512,512]{0,1:T(8,128)(2,1)S(1)} fusion(bf16[5376,512]{1,0:T(8,128)(2,1)} %param.12, bf16[1024,5376]{1,0:T(8,128)(2,1)S(1)} %constant_dynamic-update-slice_fusion, s32[]{:T(128)S(6)} %select_n.35), kind=kOutput, calls=%fused_computation.41 | convolution fusion | flops 2818834432 | bytes 11534340 | tf_op jit(solution)/shard_map/dot_general | solution.py:69
  121.6 5.1 %fusion.11 = f32[512,512]{0,1:T(8,128)S(1)} fusion(bf16[5376,512]{1,0:T(8,128)(2,1)} %param.11, bf16[1024,5376]{1,0:T(8,128)(2,1)S(1)} %constant_dynamic-update-slice_fusion, s32[]{:T(128)S(6)} %select_n.35), kind=kOutput, calls=%fused_computation.14 | convolution fusion | flops 2818572288 | bytes 12058628 | tf_op jit(solution)/shard_map/dot_general | solution.py:68
  126.7 0.2 subtract_convert_fusion
  126.9 0.1 pad_maximum_fusion
  127.0 1.4 collective-permute-start.4
  128.4 3.7 %collective-permute-start.3 = (bf16[512,1024]{0,1:T(8,128)(2,1)S(1)}, bf16[512,1024]{0,1:T(8,128)(2,1)S(1)}, u32[]{:S(2)}, u32[]{:S(2)}) collective-permute-start(bf16[512,1024]{0,1:T(8,128)(2,1)S(1)} %pad_maximum_fusion), channel_id=1, source_target_pairs={{0,8},{4,12},{8,16},{12,20},{16,24},{20,28},{1,9},{5,13},{9,17},{1... | collective-permute-start | bytes 3145736 | tf_op jit(solution)/shard_map/ppermute | solution.py:17
  132.1 8.6 %fusion.21 = f32[64,8,8,128]{3,1,2,0:T(8,128)S(1)} fusion(bf16[5376,1024]{1,0:T(8,128)(2,1)} %param.10, bf16[1024,5376]{1,0:T(8,128)(2,1)S(1)} %constant_dynamic-update-slice_fusion, s32[]{:T(128)S(6)} %select_n.35), kind=kOutput, calls=%fused_computation.39 | convolution fusion | flops 5637144576 | bytes 18612228 | tf_op jit(solution)/shard_map/dot_general | solution.py:67
  140.7 0.5 copy.23
  141.2 1.1 multiply_subtract_fusion
  142.3 0.0 copy-start.3
  142.3 0.0 copy-start.4
  142.3 0.6 fusion.20
  142.9 0.1 copy.13
  143.1 0.0 copy-start.5
  143.1 0.0 collective-permute-done.4
  143.1 12.4 %collective-permute-done.3 = bf16[512,1024]{0,1:T(8,128)(2,1)S(1)} collective-permute-done((bf16[512,1024]{0,1:T(8,128)(2,1)S(1)}, bf16[512,1024]{0,1:T(8,128)(2,1)S(1)}, u32[]{:S(2)}, u32[]{:S(2)}) %collective-permute-start.3) | collective-permute-done | bytes 1048608 | tf_op jit(solution)/shard_map/ppermute | solution.py:17
  155.4 0.0 copy-done.3
  155.4 0.0 copy-done.4
  155.4 2.2 fusion.31
  157.6 9.5 %maximum_maximum_fusion = bf16[1536,1024]{0,1:T(8,128)(2,1)S(1)} fusion(bf16[512,512]{0,1:T(8,128)(2,1)S(1)} %fusion.25, bf16[512,512]{0,1:T(8,128)(2,1)S(1)} %bitcast.48, bf16[512,1024]{0,1:T(8,128)(2,1)S(1)} %get-tuple-element.10, bf16[512,1024]{0,1:T(8,128)(2,1)S(1)} %get-tuple-element.9), kind=kLoop, calls=%fused_computation.21 | loop fusion | flops 12582912 | bytes 6291456 | tf_op jit(solution)/shard_map/concatenate | solution.py:88
  167.2 1.4 fusion.38
  168.6 0.0 copy-done.5
  168.6 11.8 %fusion.41 = f32[4,1536,512,2]{2,1,3,0:T(8,128)} fusion(bf16[1536,4,128,1]{0,2,3,1:T(8,128)(2,1)S(1)} %bitcast.45, bf16[512,4,2,128]{3,0,2,1:T(8,128)(2,1)S(1)} %bitcast.51), kind=kOutput, calls=%fused_computation.73 | convolution fusion | flops 1610612736 | bytes 27787264 | tf_op jit(solution)/shard_map/qgrd,kgd->grqk/dot_general | solution.py:98
  180.4 9.2 %fusion.40 = f32[4,2,512]{2,1,0:T(2,128)S(1)} fusion(pred[512,1536]{0,1:T(8,128)(4,1)} %fusion.13, bf16[1536,4,128,1]{0,2,3,1:T(8,128)(2,1)S(1)} %bitcast.46, bf16[512,4,2,128]{3,0,2,1:T(8,128)(2,1)} %bitcast.52), kind=kOutput, calls=%fused_computation.72 | convolution fusion | flops 1629488640 | bytes 3424256 | tf_op jit(solution)/shard_map/sub | solution.py:101
  189.6 13.0 %fusion.24 = bf16[4,128,2,512]{3,1,2,0:T(8,128)(2,1)S(1)} fusion(bf16[1536,4,128,1]{0,2,3,1:T(8,128)(2,1)} %bitcast.53, f32[4,2,512]{2,1,0:T(2,128)S(1)} %fusion.40, f32[4,1536,512,2]{2,1,3,0:T(8,128)} %fusion.41, pred[512,1536]{0,1:T(8,128)(4,1)} %fusion.13), kind=kOutput, calls=%fused_computation.40 | convolution fusion | flops 1636308480 | bytes 28590080 | tf_op jit(solution)/shard_map/grqk,kgd->qgrd/dot_general | solution.py:103
  202.6 12.1 %convolution_convert_fusion = bf16[512,5376]{1,0:T(8,128)(2,1)} fusion(bf16[512,1024]{0,1:T(8,128)(2,1)S(1)} %bitcast.55, bf16[1024,5376]{1,0:T(8,128)(2,1)} %param.13), kind=kOutput, calls=%fused_computation.8 | convolution fusion | flops 5639897088 | bytes 17563648 | tf_op jit(solution)/shard_map/dot_general | solution.py:108
  214.7 0.0 copy-start.7
  214.7 0.0 reduce-scatter.2.cloned.1.call-update
  214.7 105.5 %reduce-scatter.2.cloned.1.call-done = bf16[128,5376]{1,0:T(8,128)(2,1)} async-done(((bf16[512,5376]{1,0:T(8,128)(2,1)}), bf16[128,5376]{1,0:T(8,128)(2,1)}) %reduce-scatter.2.cloned.1.call-update) | async-done | bytes 1376272 | tf_op jit(solution)/shard_map/reduce_scatter | solution.py:107
  320.2 1.7 fusion.14
  321.9 0.0 copy-done.7
  321.9 3.0 fusion.19
  (6 shorter events, 0.1 us)
Async XLA Ops:
  6.5 313.7 %reduce-scatter.2.cloned.1.call-start = ((), (), s32[]{:S(2)}) async-start(), calls=%async_computation.1 | async-start | bytes 6881280 | tf_op jit(solution)/shard_map/reduce_scatter | solution.py:107
  10.0 35.3 %collective-permute-start = (bf16[128,5376]{1,0:T(8,128)(2,1)S(1)}, bf16[128,5376]{1,0:T(8,128)(2,1)S(1)}, u32[]{:S(2)}, u32[]{:S(2)}) collective-permute-start(bf16[128,5376]{1,0:T(8,128)(2,1)S(1)} %fusion.18), channel_id=1, source_target_pairs={{0,1},{1,2},{2,3},{3,0},{4,5},{5,6},{6,7},{7,4},{8,9},{9,10},{10,1... | collective-permute-start | bytes 4128776 | tf_op jit(solution)/shard_map/ppermute | solution.py:61
  45.3 33.2 %collective-permute-start.1 = (bf16[128,5376]{1,0:T(8,128)(2,1)S(1)}, bf16[128,5376]{1,0:T(8,128)(2,1)S(1)}, u32[]{:S(2)}, u32[]{:S(2)}) collective-permute-start(bf16[128,5376]{1,0:T(8,128)(2,1)S(1)} %collective-permute-done), channel_id=1, source_target_pairs={{0,1},{1,2},{2,3},{3,0},{4,5},{5,6},{6,7},{7,4},{8,9},{9,10},{10,1... | collective-permute-start | bytes 4128776 | tf_op jit(solution)/shard_map/ppermute | solution.py:61
  78.4 6.1 %copy-start.1 = (bf16[128,5376]{1,0:T(8,128)(2,1)}, bf16[128,5376]{1,0:T(8,128)(2,1)S(1)}, u32[]{:S(2)}) copy-start(bf16[128,5376]{1,0:T(8,128)(2,1)S(1)} %collective-permute-done.1) | copy-start | bytes 4128772
  78.4 32.3 %collective-permute-start.2 = (bf16[128,5376]{1,0:T(8,128)(2,1)S(1)}, bf16[128,5376]{1,0:T(8,128)(2,1)}, u32[]{:S(2)}, u32[]{:S(2)}) collective-permute-start(bf16[128,5376]{1,0:T(8,128)(2,1)S(1)} %collective-permute-done.1), channel_id=1, source_target_pairs={{0,1},{1,2},{2,3},{3,0},{4,5},{5,6},{6,7},{7,4},{8,9},{9,10},{10,1... | collective-permute-start | bytes 4128776 | tf_op jit(solution)/shard_map/ppermute | solution.py:61
  86.8 25.4 %copy-start.2 = (bf16[128,5376]{1,0:T(8,128)(2,1)S(1)}, bf16[128,5376]{1,0:T(8,128)(2,1)}, u32[]{:S(2)}) copy-start(bf16[128,5376]{1,0:T(8,128)(2,1)} %copy-done.1) | copy-start | bytes 4128772
  112.2 1.3 copy-start
  112.2 1.3 copy-start.6
  127.0 16.1 %collective-permute-start.4 = (bf16[512,1024]{0,1:T(8,128)(2,1)S(1)}, bf16[512,1024]{0,1:T(8,128)(2,1)S(1)}, u32[]{:S(2)}, u32[]{:S(2)}) collective-permute-start(bf16[512,1024]{0,1:T(8,128)(2,1)S(1)} %pad_maximum_fusion), channel_id=1, source_target_pairs={{0,4},{4,8},{8,12},{12,16},{16,20},{20,24},{24,28},{1,5},{5,9},{9,... | collective-permute-start | bytes 3145736 | tf_op jit(solution)/shard_map/ppermute | solution.py:17
  128.4 27.1 %collective-permute-start.3 = (bf16[512,1024]{0,1:T(8,128)(2,1)S(1)}, bf16[512,1024]{0,1:T(8,128)(2,1)S(1)}, u32[]{:S(2)}, u32[]{:S(2)}) collective-permute-start(bf16[512,1024]{0,1:T(8,128)(2,1)S(1)} %pad_maximum_fusion), channel_id=1, source_target_pairs={{0,8},{4,12},{8,16},{12,20},{16,24},{20,28},{1,9},{5,13},{9,17},{1... | collective-permute-start | bytes 3145736 | tf_op jit(solution)/shard_map/ppermute | solution.py:17
  142.3 13.2 %copy-start.3 = (bf16[1,1024,512]{1,2,0:T(8,128)(2,1)S(1)}, bf16[1,1024,512]{1,2,0:T(8,128)(2,1)}, u32[]{:S(2)}) copy-start(bf16[1,1024,512]{1,2,0:T(8,128)(2,1)} %copy.22) | copy-start | bytes 3145732
  142.3 13.2 %copy-start.4 = (bf16[1,1024,512]{1,2,0:T(8,128)(2,1)S(1)}, bf16[1,1024,512]{1,2,0:T(8,128)(2,1)}, u32[]{:S(2)}) copy-start(bf16[1,1024,512]{1,2,0:T(8,128)(2,1)} %copy.21) | copy-start | bytes 3145732
  143.1 25.5 %copy-start.5 = (bf16[512,8,128]{2,0,1:T(8,128)(2,1)}, bf16[512,8,128]{2,0,1:T(8,128)(2,1)S(1)}, u32[]{:S(2)}) copy-start(bf16[512,8,128]{2,0,1:T(8,128)(2,1)S(1)} %copy.13) | copy-start | bytes 3145732
  214.7 107.2 %copy-start.7 = (f32[5376]{0:T(1024)S(1)}, f32[5376]{0:T(1024)}, u32[]{:S(2)}) copy-start(f32[5376]{0:T(1024)} %param.15) | copy-start | bytes 64516
Sparse Core Ops, SparseCore 0:
  214.8 105.3 reduce-scatter.1
